TPU v7x, 256 devices: a whole 4x4x8 slice. The times are simulated.
256 devices in a mesh: blk: 64 (over x_lo, y, z), group: 4 (over x_hi, core).
Axes of the slice: x: 4 (x_hi: 2, x_lo: 2; x = x_hi * 2 + x_lo), y: 4, z: 8, core: 2. Of those that a mesh axis runs over, the one named last changes fastest.
Arguments:
- image: float32 [8192, 1152], P(('blk', 'group')), may hold values from -6 to 6
- text: float32 [8192, 1152], P(('blk', 'group')), may hold values from -6 to 6
- image_ids: int32 [8192], P(('blk', 'group')), may hold values from 0 to 1023
- text_ids: int32 [8192], P(('blk', 'group')), may hold values from 0 to 1023
- log_scale: float32 [1], replicated, may hold values from -4.1 to -3
- bias: float32 [1], replicated, may hold values from -2 to 0
Outputs:
- grad_image: float32 [8192, 1152], P(('blk', 'group'))
- grad_text: float32 [8192, 1152], P(('blk', 'group'))
- statistics: float32 [3], replicated
All inputs are finite; a program needn't handle non-finite values.
Results may differ from a plain program's by a relative error of at most 0.0003.
Values sent between devices are 32-bit elements; how exact they have to be, the bound alone decides.
No kernel may reach another device: no remote copies, remote signals or barrier semaphores. Data moves between devices by JAX's collectives and lax.ppermute only.
A program may use at most 128 MiB of HBM per device.

v0:
```python
import jax
import jax.numpy as jnp
from jax import lax
from jax.experimental import pallas as pl
from jax.experimental.pallas import tpu as pltpu
from jax.sharding import PartitionSpec as P

AXES = ("blk", "group")
NX, NY, NZ = 4, 4, 8
ROWS, D = 32, 1152
COLS = D // 128
MSG = ROWS // 8 * COLS + 1
HALF = ROWS // 16 * COLS
SIDE = 512
F32, BF16 = jnp.float32, jnp.bfloat16


def spot(x, y, z, c):
    return (((x % 2) * NY + y) * NZ + z) * 4 + (x // 2) * 2 + c


def table(move):
    pairs = []
    for x in range(NX):
        for y in range(NY):
            for z in range(NZ):
                for c in range(2):
                    a, b, d, e = move(x, y, z, c)
                    pairs.append((spot(x, y, z, c), spot(a % NX, b % NY, d % NZ, e)))
    return pairs


SWAP = table(lambda x, y, z, c: (x, y, z, 1 - c))


def along_z(way):
    return table(lambda x, y, z, c: (x, y, z + (way if c == 0 else -way), c))


def first(way):
    return table(lambda x, y, z, c: (x + way, y, z, c) if c == 0 else (x, y + way, z, c))


def second(way):
    return table(lambda x, y, z, c: (x, y + way, z, c) if c == 0 else (x + way, y, z, c))


def send(block, route):
    return lax.ppermute(block, AXES, route)


def pack(image_ref, text_ref, image_ids_ref, text_ids_ref, image_out, text_out):
    for rows, ids, out in ((image_ref, image_ids_ref, image_out), (text_ref, text_ids_ref, text_out)):
        for r in range(ROWS // 8):
            for c in range(COLS):
                at = r * COLS + c
                out[at + (1 if at >= HALF else 0)] = rows[8 * r : 8 * r + 8, 128 * c : 128 * c + 128]
        out[HALF] = jnp.zeros((8, 128), F32)
        out[HALF, 0:1, 0:ROWS] = ids[...].astype(F32)


def whole(operand, block):
    at = block * MSG
    return [(operand, at, at + HALF, 0, 16), (operand, at + HALF + 1, at + HALF, 16, 16)]


IMAGE_SIZES = (64, 64, 64, 64, 32, 64, 64, 64, 32)
TEXT_SIZES = (128, 128, 128, 64, 64)
IMAGE_PARTS = [part for k, size in enumerate(IMAGE_SIZES) for b in range(size // 32) for part in whole(k, b)]
TEXT_PARTS = [part for k, size in enumerate(TEXT_SIZES) for b in range(size // 32) for part in whole(k, b)]
IMAGE_STARTS = tuple(sum(IMAGE_SIZES[:k]) for k in range(len(IMAGE_SIZES)))
TEXT_STARTS = tuple(sum(TEXT_SIZES[:k]) for k in range(len(TEXT_SIZES)))
PIECES = range(len(IMAGE_SIZES))
N_IMAGE, N_TEXT = len(IMAGE_SIZES), len(TEXT_SIZES)


def split(value):
    high = value.astype(BF16)
    return high, (value - high.astype(F32)).astype(BF16)


def fill(refs, parts, high, low, row):
    start = 0
    for operand, at, tag, lane, rows in parts:
        ref = refs[operand]
        for c in range(COLS):
            piece = jnp.concatenate([ref[at + c], ref[at + COLS + c]], axis=0)
            a, b = split(piece)
            high[start : start + 16, 128 * c : 128 * c + 128] = a
            low[start : start + 16, 128 * c : 128 * c + 128] = b
        row[0:1, start : start + rows] = ref[tag, 0:1, lane : lane + rows]
        start += rows


def dot3(a, b, dims):
    def one(p, q):
        return lax.dot_general(p, q, (dims, ((), ())), preferred_element_type=F32)

    return one(a[0], b[0]) + (one(a[0], b[1]) + one(a[1], b[0]))


CHUNK = 256


def emit(out, rows, sums):
    for r in range(rows.shape[0] // 8):
        for c in range(COLS):
            at = r * COLS + c
            out[at + (1 if r >= ROWS // 8 else 0)] = rows[8 * r : 8 * r + 8, 128 * c : 128 * c + 128]
    out[MSG - 1] = sums


def gradients(image_pieces, text_pieces, held, sums, outs):
    ih, il, th, tl, wh, wl = held
    for group in ((0, 1, 2, 3), (4, 5, 6, 7, 8)):
        at = IMAGE_STARTS[group[0]]
        rows = slice(at, at + sum(IMAGE_SIZES[k] for k in group))
        terms = dot3((wh[rows, :], wl[rows, :]), (th[...], tl[...]), ((1,), (0,)))
        for k in group:
            first_row = IMAGE_STARTS[k] - at
            share = 0.5 if IMAGE_SIZES[k] == 32 else 1.0
            emit(outs[k], terms[first_row : first_row + IMAGE_SIZES[k], :], share * sums)
    outs = outs[len(image_pieces) :]
    for group in ((0, 1), (2, 3, 4)):
        at = TEXT_STARTS[group[0]]
        cols = slice(at, at + sum(TEXT_SIZES[k] for k in group))
        terms = dot3((wh[:, cols], wl[:, cols]), (ih[...], il[...]), ((0,), (0,)))
        for k in group:
            first_row = TEXT_STARTS[k] - at
            outs[k][...] = terms[first_row : first_row + TEXT_SIZES[k], :]


def visit(image_pieces, text_pieces, *refs):
    log_scale_ref, bias_ref, place_ref = refs[:3]
    refs = refs[3:]
    image_refs = refs[:N_IMAGE]
    text_refs = refs[N_IMAGE : N_IMAGE + N_TEXT]
    sums_ref, *outs, ih, il, th, tl, wh, wl, irow, trow = refs[N_IMAGE + N_TEXT :]
    fill(image_refs, IMAGE_PARTS, ih, il, irow)
    fill(text_refs, TEXT_PARTS, th, tl, trow)
    scale = jnp.exp(log_scale_ref[...])
    offset = bias_ref[...]
    tags = jnp.transpose(jnp.broadcast_to(irow[0:1, :], (128, SIDE)))
    text_tags = trow[0:1, :]
    losses_sum = jnp.zeros((8, 128), F32)
    moment_sum = jnp.zeros((8, 128), F32)
    slope_sum = jnp.zeros((8, 128), F32)

    def fold(v):
        return jnp.sum(v.reshape(CHUNK // 8, 8, 128), axis=0)

    for k in range(SIDE // CHUNK):
        rows = slice(k * CHUNK, (k + 1) * CHUNK)
        dots = dot3((ih[rows, :], il[rows, :]), (th[...], tl[...]), ((1,), (1,)))
        for j in range(SIDE // 128):
            lanes = slice(128 * j, 128 * j + 128)
            moved = scale * dots[:, lanes]
            logits = moved + offset
            same = tags[rows, :] == text_tags[:, lanes]
            v = jnp.where(same, -logits, logits)
            e = jnp.exp(-jnp.abs(v))
            u = 1.0 + e
            r = 1.0 / u
            losses = jnp.maximum(v, 0.0) + (jnp.log(u) + (e - (u - 1.0)) * r)
            sig = jnp.where(v >= 0.0, r, e * r)
            slope = jnp.where(same, -sig, sig)
            losses_sum += fold(losses)
            moment_sum += fold(slope * moved)
            slope_sum += fold(slope)
            a, b = split(scale * slope)
            wh[rows, lanes] = a
            wl[rows, lanes] = b
    row = lax.broadcasted_iota(jnp.int32, (8, 128), 0)
    lane = lax.broadcasted_iota(jnp.int32, (8, 128), 1)
    mine = lane + 128 * (row % 2) == place_ref[...]
    sums = jnp.zeros((8, 128), F32)
    for k, total in enumerate((losses_sum, moment_sum, slope_sum)):
        sums = jnp.where(mine & (row // 2 == k), jnp.sum(total, keepdims=True), sums)
    sums_ref[...] = sums
    gradients(image_pieces, text_pieces, (ih, il, th, tl, wh, wl), sums, outs)


def unpack(kept_ref, came_ref, other_ref, after_ref, rows_out, sums_out):
    for r in range(ROWS // 8):
        for c in range(COLS):
            at = r * COLS + c
            rows_out[8 * r : 8 * r + 8, 128 * c : 128 * c + 128] = kept_ref[at] + came_ref[at] + other_ref[1 + at]
    sums_out[...] = kept_ref[MSG - 1] + came_ref[MSG - 1] + other_ref[0]


def tiles(count):
    return jax.ShapeDtypeStruct((count, 8, 128), F32)


def rows_of(count):
    return jax.ShapeDtypeStruct((count, D), F32)


def vmem(count):
    return [pl.BlockSpec(memory_space=pltpu.VMEM)] * count


def cost(products, operands):
    return pl.CostEstimate(flops=6 * products, bytes_accessed=operands, transcendentals=0)


def shapes_of(image_pieces, text_pieces):
    return tuple(tiles(IMAGE_SIZES[k] // 8 * COLS + 1) for k in image_pieces) + tuple(
        rows_of(TEXT_SIZES[k]) for k in text_pieces
    )


def behind(first_block, *blocks):
    anywhere = pl.BlockSpec(memory_space=pl.ANY)
    return pl.pallas_call(
        lambda *refs: None,
        out_shape=tuple(jax.ShapeDtypeStruct(block.shape, block.dtype) for block in blocks),
        in_specs=[anywhere] * (1 + len(blocks)),
        out_specs=(anywhere,) * len(blocks),
        input_output_aliases={1 + n: n for n in range(len(blocks))},
        compiler_params=pltpu.CompilerParams(vmem_limit_bytes=2**20),
    )(first_block, *blocks)


def put(block, top, bottom):
    return jnp.pad(block, ((top, bottom),) + ((0, 0),) * (block.ndim - 1))


def shards(image, text, image_ids, text_ids, log_scale, bias):
    i0, t0 = pl.pallas_call(
        pack,
        out_shape=(tiles(MSG), tiles(MSG)),
        in_specs=vmem(4),
        out_specs=tuple(vmem(2)),
    )(image, text, image_ids.reshape(1, ROWS), text_ids.reshape(1, ROWS))

    c0 = jnp.concatenate([i0, send(i0, SWAP)], axis=0)
    z1 = send(c0, along_z(1))
    a = send(t0, first(1))
    b = send(t0, first(-1))
    c = send(t0, first(2))
    y0 = jnp.concatenate([t0, a, b, c], axis=0)
    z2 = send(z1, along_z(1))
    s1 = send(z1, SWAP)
    yp = send(y0, second(1))
    ym = send(y0, second(-1))
    z3 = send(z2, along_z(1))
    s2 = send(z2, SWAP)
    y2a = send(yp[: 2 * MSG], second(1))
    y2b = send(ym[2 * MSG :], second(-1))
    z4 = send(z3[:MSG], along_z(1))
    s3 = send(z3, SWAP)
    s4 = send(z4, SWAP)

    early = shapes_of(PIECES, range(N_TEXT))
    place = lax.axis_index("blk") * 4 + lax.axis_index("group")
    *_, gc, g1, g2, g3, g4, h1, h2, h3, h4, k0, kp, km, k2a, k2b = pl.pallas_call(
        lambda *refs: visit(PIECES, range(N_TEXT), *refs),
        out_shape=(jax.ShapeDtypeStruct((8, 128), F32),) + early,
        in_specs=vmem(3 + N_IMAGE + N_TEXT),
        out_specs=tuple(vmem(1 + len(early))),
        scratch_shapes=[pltpu.VMEM((SIDE, D), BF16)] * 4
        + [pltpu.VMEM((SIDE, SIDE), BF16)] * 2
        + [pltpu.VMEM((8, SIDE), F32)] * 2,
        compiler_params=pltpu.CompilerParams(vmem_limit_bytes=40 * 2**20),
        cost_estimate=cost(3 * SIDE * SIDE * D, 8 * SIDE * D),
    )(
        log_scale.reshape(1, 1), bias.reshape(1, 1), place.reshape(1, 1),
        c0, z1, z2, z3, z4, s1, s2, s3, s4,
        y0, yp, ym, y2a, y2b,
    )

    q4 = send(h4, SWAP)
    g4 = g4 + q4
    w4 = send(g4, along_z(-1))
    k2a, k2b = behind(g4, k2a, k2b)
    r2a = send(k2a, second(-1))
    r2b = send(k2b, second(1))
    q3 = send(h3, SWAP)
    w3 = send(g3 + q3 + put(w4, 0, MSG - 1), along_z(-1))
    rp = send(kp + put(r2a, 0, 64), second(-1))
    rm = send(km + put(r2b, 64, 0), second(1))
    q2 = send(h2, SWAP)
    q1 = send(h1, SWAP)
    w2 = send(g2 + q2 + w3, along_z(-1))
    w1 = send(g1 + q1 + w2, along_z(-1))
    k0 = k0 + rp + rm
    ra = send(k0[32:64], first(-1))
    rb = send(k0[64:96], first(1))
    rc = send(k0[96:128], first(2))
    grad_text = k0[:32] + ra + rb + rc
    other = send(gc[MSG - 1 :] + w1[MSG - 1 :], SWAP)
    grad_image, sums = pl.pallas_call(
        unpack,
        out_shape=(rows_of(ROWS), jax.ShapeDtypeStruct((8, 128), F32)),
        in_specs=vmem(3) + [pl.BlockSpec(memory_space=pl.ANY)],
        out_specs=tuple(vmem(2)),
        compiler_params=pltpu.CompilerParams(vmem_limit_bytes=2 * 2**20),
    )(gc, w1, other, ra)
    lines = [[spot(x, y, z, c) for x in range(NX) for y in range(NY)] for z in range(NZ) for c in range(2)]
    every = lax.all_to_all(
        jnp.broadcast_to(sums, (NX * NY, 8, 128)), AXES, 0, 0, axis_index_groups=lines, tiled=True
    )
    statistics = jnp.sum(every[:, :6].reshape(NX * NY, 3, 256), axis=(0, 2)) * (2.0**-26)
    return grad_image, grad_text, statistics


def solution(mesh):
    rows, ids = P(AXES, None), P(AXES)
    return jax.shard_map(
        shards,
        mesh=mesh,
        in_specs=(rows, rows, ids, ids, P(), P()),
        out_specs=(rows, rows, P()),
        check_vma=False,
    )
```

profile of v0, /device:TPU:96, one launch (start us, length us, event | category | flops | bytes accessed | tf_op | source)
XLA Modules:
  0.0 105.0 jit_solution(17372560382404561590)
XLA Ops:
  0.6 1.7 %shard_map.85 = (f32[37,8,128]{2,1,0:T(8,128)}, f32[37,8,128]{2,1,0:T(8,128)}) custom-call(f32[32,1152]{1,0:T(8,128)} %image_ref.1, f32[32,1152]{1,0:T(8,128)} %text_ref.1, s32[1,32]{1,0:T(1,128)} %bitcast.7, s32[1,32]{1,0:T(1,128)} %bitcast.8), custom_call_target="tpu_custom_call" | custom-call | tf_op jit(solution)/shard_map/pallas_call | solution.py:230
  2.4 3.0 %collective-permute-start.11 = (f32[37,8,128]{2,1,0:T(8,128)}, f32[37,8,128]{2,1,0:T(8,128)S(1)}, u32[]{:S(2)}, u32[]{:S(2)}) collective-permute-start(f32[37,8,128]{2,1,0:T(8,128)} %get-tuple-element.24), channel_id=1, source_target_pairs={{0,2},{1,65},{4,6},{5,69},{8,10},{9,73},{12,14},{13,77},{16,18},{1... | collective-permute-start | bytes 454664 | tf_op jit(solution)/shard_map/ppermute | solution.py:49
  5.4 1.1 %collective-permute-start.10 = (f32[37,8,128]{2,1,0:T(8,128)}, f32[37,8,128]{2,1,0:T(8,128)S(1)}, u32[]{:S(2)}, u32[]{:S(2)}) collective-permute-start(f32[37,8,128]{2,1,0:T(8,128)} %get-tuple-element.24), channel_id=1, source_target_pairs={{0,130},{1,97},{4,134},{5,101},{8,138},{9,105},{12,142},{13,109},{... | collective-permute-start | bytes 454664 | tf_op jit(solution)/shard_map/ppermute | solution.py:49
  9.0 3.2 %collective-permute-start.1 = (f32[74,8,128]{2,1,0:T(8,128)S(1)}, f32[74,8,128]{2,1,0:T(8,128)S(1)}, u32[]{:S(2)}, u32[]{:S(2)}) collective-permute-start(f32[74,8,128]{2,1,0:T(8,128)S(1)} %constant_dynamic-update-slice_fusion.refs_3_), channel_id=1, source_target_pairs={{0,4},{1,29},{4,8},{5,1},{8,12},{9,5},{12,16},{13,9},{16,20},{17,1... | collective-permute-start | bytes 909320 | tf_op jit(solution)/shard_map/ppermute | solution.py:49
  13.2 3.1 %collective-permute-start.13 = (f32[148,8,128]{2,1,0:T(8,128)S(1)}, f32[148,8,128]{2,1,0:T(8,128)S(1)}, u32[]{:S(2)}, u32[]{:S(2)}) collective-permute-start(f32[148,8,128]{2,1,0:T(8,128)S(1)} %constant_dynamic-update-slice_fusion.2.refs_12_), channel_id=1, source_target_pairs={{0,96},{1,131},{4,100},{5,135},{8,104},{9,139},{12,108},{13,143},{... | collective-permute-start | bytes 1818632 | tf_op jit(solution)/shard_map/ppermute | solution.py:49
  16.6 3.7 %collective-permute-start.2 = (f32[74,8,128]{2,1,0:T(8,128)S(1)}, f32[74,8,128]{2,1,0:T(8,128)S(1)}, u32[]{:S(2)}, u32[]{:S(2)}) collective-permute-start(f32[74,8,128]{2,1,0:T(8,128)S(1)} %collective-permute-done.1.refs_4_), channel_id=1, source_target_pairs={{0,4},{1,29},{4,8},{5,1},{8,12},{9,5},{12,16},{13,9},{16,20},{17,1... | collective-permute-start | bytes 909320 | tf_op jit(solution)/shard_map/ppermute | solution.py:49
  20.2 4.3 %collective-permute-done.2.refs_5_ = f32[74,8,128]{2,1,0:T(8,128)S(1)} collective-permute-done((f32[74,8,128]{2,1,0:T(8,128)S(1)}, f32[74,8,128]{2,1,0:T(8,128)S(1)}, u32[]{:S(2)}, u32[]{:S(2)}) %collective-permute-start.2) | collective-permute-done | bytes 303136 | tf_op jit(solution)/shard_map/ppermute | solution.py:49
  24.6 3.7 %collective-permute-start.3 = (f32[74,8,128]{2,1,0:T(8,128)S(1)}, f32[74,8,128]{2,1,0:T(8,128)S(1)}, u32[]{:S(2)}, u32[]{:S(2)}) collective-permute-start(f32[74,8,128]{2,1,0:T(8,128)S(1)} %collective-permute-done.2.refs_5_), channel_id=1, source_target_pairs={{0,4},{1,29},{4,8},{5,1},{8,12},{9,5},{12,16},{13,9},{16,20},{17,1... | collective-permute-start | bytes 909320 | tf_op jit(solution)/shard_map/ppermute | solution.py:49
  29.5 3.0 %collective-permute-start.15 = (f32[74,8,128]{2,1,0:T(8,128)}, f32[74,8,128]{2,1,0:T(8,128)}, u32[]{:S(2)}, u32[]{:S(2)}) collective-permute-start(f32[74,8,128]{2,1,0:T(8,128)} %slice.42), channel_id=1, source_target_pairs={{0,96},{1,131},{4,100},{5,135},{8,104},{9,139},{12,108},{13,143},{... | collective-permute-start | bytes 909320 | tf_op jit(solution)/shard_map/ppermute | solution.py:49
  33.3 3.0 %collective-permute-start.4 = (f32[37,8,128]{2,1,0:T(8,128)S(1)}, f32[37,8,128]{2,1,0:T(8,128)S(1)}, u32[]{:S(2)}, u32[]{:S(2)}) collective-permute-start(f32[37,8,128]{2,1,0:T(8,128)S(1)} %slice.40), channel_id=1, source_target_pairs={{0,4},{1,29},{4,8},{5,1},{8,12},{9,5},{12,16},{13,9},{16,20},{17,1... | collective-permute-start | bytes 454664 | tf_op jit(solution)/shard_map/ppermute | solution.py:49
  36.4 2.7 %collective-permute-done.4.refs_7_ = f32[37,8,128]{2,1,0:T(8,128)S(1)} collective-permute-done((f32[37,8,128]{2,1,0:T(8,128)S(1)}, f32[37,8,128]{2,1,0:T(8,128)S(1)}, u32[]{:S(2)}, u32[]{:S(2)}) %collective-permute-start.4) | collective-permute-done | bytes 151584 | tf_op jit(solution)/shard_map/ppermute | solution.py:49
  40.4 1.2 %collective-permute-done.14.refs_15_ = f32[74,8,128]{2,1,0:T(8,128)} collective-permute-done((f32[74,8,128]{2,1,0:T(8,128)}, f32[74,8,128]{2,1,0:T(8,128)}, u32[]{:S(2)}, u32[]{:S(2)}) %collective-permute-start.14) | collective-permute-done | bytes 303136 | tf_op jit(solution)/shard_map/ppermute | solution.py:49
  41.7 8.8 %shard_map.86 = (f32[8,128]{1,0:T(8,128)}, f32[73,8,128]{2,1,0:T(8,128)S(1)}, f32[73,8,128]{2,1,0:T(8,128)S(1)}, f32[73,8,128]{2,1,0:T(8,128)S(1)}, f32[73,8,128...) custom-call(f32[1,1]{1,0:T(1,128)} %bitcast.5.refs_0_, ...), custom_call_target="tpu_custom_call" | custom-call | flops 5435817984 | bytes 4718592 | tf_op jit(solution)/shard_map/pallas_call | solution.py:257
  52.7 2.4 %collective-permute-start.16 = (f32[73,8,128]{2,1,0:T(8,128)S(1)}, f32[73,8,128]{2,1,0:T(8,128)S(1)}, u32[]{:S(2)}, u32[]{:S(2)}) collective-permute-start(f32[73,8,128]{2,1,0:T(8,128)S(1)} %get-tuple-element.27), channel_id=1, source_target_pairs={{0,1},{1,0},{4,5},{5,4},{8,9},{9,8},{12,13},{13,12},{16,17},{17,16... | collective-permute-start | bytes 897032 | tf_op jit(solution)/shard_map/ppermute | solution.py:49
  55.1 3.0 %collective-permute-start.25 = (f32[64,1152]{1,0:T(8,128)S(1)}, f32[64,1152]{1,0:T(8,128)S(1)}, u32[]{:S(2)}, u32[]{:S(2)}) collective-permute-start(f32[64,1152]{1,0:T(8,128)S(1)} %get-tuple-element.38), channel_id=1, source_target_pairs={{0,96},{1,131},{4,100},{5,135},{8,104},{9,139},{12,108},{13,143},{... | collective-permute-start | bytes 884744 | tf_op jit(solution)/shard_map/ppermute | solution.py:49
  58.6 1.5 %collective-permute-done.27 = f32[64,1152]{1,0:T(8,128)S(1)} collective-permute-done((f32[64,1152]{1,0:T(8,128)S(1)}, f32[64,1152]{1,0:T(8,128)S(1)}, u32[]{:S(2)}, u32[]{:S(2)}) %collective-permute-start.27) | collective-permute-done | bytes 294944 | tf_op jit(solution)/shard_map/ppermute | solution.py:49
  60.4 1.9 %collective-permute-done.25 = f32[64,1152]{1,0:T(8,128)S(1)} collective-permute-done((f32[64,1152]{1,0:T(8,128)S(1)}, f32[64,1152]{1,0:T(8,128)S(1)}, u32[]{:S(2)}, u32[]{:S(2)}) %collective-permute-start.25) | collective-permute-done | bytes 294944 | tf_op jit(solution)/shard_map/ppermute | solution.py:49
  62.4 3.8 %collective-permute-start.26 = (f32[128,1152]{1,0:T(8,128)S(1)}, f32[128,1152]{1,0:T(8,128)S(1)}, u32[]{:S(2)}, u32[]{:S(2)}) collective-permute-start(f32[128,1152]{1,0:T(8,128)S(1)} %pad_add_fusion.1), channel_id=1, source_target_pairs={{0,96},{1,131},{4,100},{5,135},{8,104},{9,139},{12,108},{13,143},{... | collective-permute-start | bytes 1769480 | tf_op jit(solution)/shard_map/ppermute | solution.py:49
  66.7 8.0 %collective-permute-done.22 = f32[73,8,128]{2,1,0:T(8,128)S(1)} collective-permute-done((f32[73,8,128]{2,1,0:T(8,128)S(1)}, f32[73,8,128]{2,1,0:T(8,128)S(1)}, u32[]{:S(2)}, u32[]{:S(2)}) %collective-permute-start.22) | collective-permute-done | bytes 299040 | tf_op jit(solution)/shard_map/ppermute | solution.py:49
  74.9 7.8 %collective-permute-done.23.came_ref = f32[73,8,128]{2,1,0:T(8,128)S(1)} collective-permute-done((f32[73,8,128]{2,1,0:T(8,128)S(1)}, f32[73,8,128]{2,1,0:T(8,128)S(1)}, u32[]{:S(2)}, u32[]{:S(2)}) %collective-permute-start.23) | collective-permute-done | bytes 299040 | tf_op jit(solution)/shard_map/ppermute | solution.py:49
  82.9 2.4 %collective-permute-start.29 = (f32[32,1152]{1,0:T(8,128)S(1)}, f32[32,1152]{1,0:T(8,128)S(1)}, u32[]{:S(2)}, u32[]{:S(2)}) collective-permute-start(f32[32,1152]{1,0:T(8,128)S(1)} %get-tuple-element.45), channel_id=1, source_target_pairs={{0,130},{1,97},{4,134},{5,101},{8,138},{9,105},{12,142},{13,109},{... | collective-permute-start | bytes 442376 | tf_op jit(solution)/shard_map/ppermute | solution.py:49
  85.3 2.6 %collective-permute-start.31 = (f32[32,1152]{1,0:T(8,128)S(1)}, f32[32,1152]{1,0:T(8,128)S(1)}, u32[]{:S(2)}, u32[]{:S(2)}) collective-permute-start(f32[32,1152]{1,0:T(8,128)S(1)} %get-tuple-element.44), channel_id=1, source_target_pairs={{0,2},{1,65},{4,6},{5,69},{8,10},{9,73},{12,14},{13,77},{16,18},{1... | collective-permute-start | bytes 442376 | tf_op jit(solution)/shard_map/ppermute | solution.py:49
  89.5 7.0 %all-to-all-start = ((f32[16,8,128]{2,1,0:T(8,128)}), f32[16,8,128]{2,1,0:T(8,128)S(1)}, u32[]{:S(2)}, u32[]{:S(2)}) async-start(f32[16,8,128]{2,1,0:T(8,128)} %broadcast_in_dim.3), calls=%async_computation | async-start | bytes 131072 | tf_op jit(solution)/shard_map/all_to_all | solution.py:301
  97.2 7.0 %all-to-all-done = f32[16,8,128]{2,1,0:T(8,128)S(1)} async-done(((f32[16,8,128]{2,1,0:T(8,128)}), f32[16,8,128]{2,1,0:T(8,128)S(1)}, u32[]{:S(2)}, u32[]{:S(2)}) %all-to-all-start) | async-done | bytes 65568 | tf_op jit(solution)/shard_map/all_to_all | solution.py:301
  (72 shorter events, 12.8 us)
Async XLA Ops:
  2.4 10.8 %collective-permute-start.11 = (f32[37,8,128]{2,1,0:T(8,128)}, f32[37,8,128]{2,1,0:T(8,128)S(1)}, u32[]{:S(2)}, u32[]{:S(2)}) collective-permute-start(f32[37,8,128]{2,1,0:T(8,128)} %get-tuple-element.24), channel_id=1, source_target_pairs={{0,2},{1,65},{4,6},{5,69},{8,10},{9,73},{12,14},{13,77},{16,18},{1... | collective-permute-start | bytes 454664 | tf_op jit(solution)/shard_map/ppermute | solution.py:49
  5.4 7.8 %collective-permute-start.10 = (f32[37,8,128]{2,1,0:T(8,128)}, f32[37,8,128]{2,1,0:T(8,128)S(1)}, u32[]{:S(2)}, u32[]{:S(2)}) collective-permute-start(f32[37,8,128]{2,1,0:T(8,128)} %get-tuple-element.24), channel_id=1, source_target_pairs={{0,130},{1,97},{4,134},{5,101},{8,138},{9,105},{12,142},{13,109},{... | collective-permute-start | bytes 454664 | tf_op jit(solution)/shard_map/ppermute | solution.py:49
  6.5 6.6 %collective-permute-start.9 = (f32[37,8,128]{2,1,0:T(8,128)}, f32[37,8,128]{2,1,0:T(8,128)S(1)}, u32[]{:S(2)}, u32[]{:S(2)}) collective-permute-start(f32[37,8,128]{2,1,0:T(8,128)} %get-tuple-element.24), channel_id=1, source_target_pairs={{0,128},{1,33},{4,132},{5,37},{8,136},{9,41},{12,140},{13,45},{16,... | collective-permute-start | bytes 454664 | tf_op jit(solution)/shard_map/ppermute | solution.py:49
  9.0 7.5 %collective-permute-start.1 = (f32[74,8,128]{2,1,0:T(8,128)S(1)}, f32[74,8,128]{2,1,0:T(8,128)S(1)}, u32[]{:S(2)}, u32[]{:S(2)}) collective-permute-start(f32[74,8,128]{2,1,0:T(8,128)S(1)} %constant_dynamic-update-slice_fusion.refs_3_), channel_id=1, source_target_pairs={{0,4},{1,29},{4,8},{5,1},{8,12},{9,5},{12,16},{13,9},{16,20},{17,1... | collective-permute-start | bytes 909320 | tf_op jit(solution)/shard_map/ppermute | solution.py:49
  13.2 15.6 %collective-permute-start.13 = (f32[148,8,128]{2,1,0:T(8,128)S(1)}, f32[148,8,128]{2,1,0:T(8,128)S(1)}, u32[]{:S(2)}, u32[]{:S(2)}) collective-permute-start(f32[148,8,128]{2,1,0:T(8,128)S(1)} %constant_dynamic-update-slice_fusion.2.refs_12_), channel_id=1, source_target_pairs={{0,96},{1,131},{4,100},{5,135},{8,104},{9,139},{12,108},{13,143},{... | collective-permute-start | bytes 1818632 | tf_op jit(solution)/shard_map/ppermute | solution.py:49
  16.3 16.2 %collective-permute-start.12 = (f32[148,8,128]{2,1,0:T(8,128)S(1)}, f32[148,8,128]{2,1,0:T(8,128)S(1)}, u32[]{:S(2)}, u32[]{:S(2)}) collective-permute-start(f32[148,8,128]{2,1,0:T(8,128)S(1)} %constant_dynamic-update-slice_fusion.2.refs_12_), channel_id=1, source_target_pairs={{0,32},{1,129},{4,36},{5,133},{8,40},{9,137},{12,44},{13,141},{16,... | collective-permute-start | bytes 1818632 | tf_op jit(solution)/shard_map/ppermute | solution.py:49
  16.6 8.0 %collective-permute-start.2 = (f32[74,8,128]{2,1,0:T(8,128)S(1)}, f32[74,8,128]{2,1,0:T(8,128)S(1)}, u32[]{:S(2)}, u32[]{:S(2)}) collective-permute-start(f32[74,8,128]{2,1,0:T(8,128)S(1)} %collective-permute-done.1.refs_4_), channel_id=1, source_target_pairs={{0,4},{1,29},{4,8},{5,1},{8,12},{9,5},{12,16},{13,9},{16,20},{17,1... | collective-permute-start | bytes 909320 | tf_op jit(solution)/shard_map/ppermute | solution.py:49
  24.6 8.7 %collective-permute-start.3 = (f32[74,8,128]{2,1,0:T(8,128)S(1)}, f32[74,8,128]{2,1,0:T(8,128)S(1)}, u32[]{:S(2)}, u32[]{:S(2)}) collective-permute-start(f32[74,8,128]{2,1,0:T(8,128)S(1)} %collective-permute-done.2.refs_5_), channel_id=1, source_target_pairs={{0,4},{1,29},{4,8},{5,1},{8,12},{9,5},{12,16},{13,9},{16,20},{17,1... | collective-permute-start | bytes 909320 | tf_op jit(solution)/shard_map/ppermute | solution.py:49
  28.3 8.1 %collective-permute-start.5 = (f32[74,8,128]{2,1,0:T(8,128)S(1)}, f32[74,8,128]{2,1,0:T(8,128)S(1)}, u32[]{:S(2)}, u32[]{:S(2)}) collective-permute-start(f32[74,8,128]{2,1,0:T(8,128)S(1)} %collective-permute-done.1.refs_4_), channel_id=1, source_target_pairs={{0,1},{1,0},{4,5},{5,4},{8,9},{9,8},{12,13},{13,12},{16,17},{17,16... | collective-permute-start | bytes 909320 | tf_op jit(solution)/shard_map/ppermute | solution.py:49
  28.3 12.1 %collective-permute-start.6 = (f32[74,8,128]{2,1,0:T(8,128)S(1)}, f32[74,8,128]{2,1,0:T(8,128)}, u32[]{:S(2)}, u32[]{:S(2)}) collective-permute-start(f32[74,8,128]{2,1,0:T(8,128)S(1)} %collective-permute-done.2.refs_5_), channel_id=1, source_target_pairs={{0,1},{1,0},{4,5},{5,4},{8,9},{9,8},{12,13},{13,12},{16,17},{17,16... | collective-permute-start | bytes 909320 | tf_op jit(solution)/shard_map/ppermute | solution.py:49
  29.5 10.9 %collective-permute-start.15 = (f32[74,8,128]{2,1,0:T(8,128)}, f32[74,8,128]{2,1,0:T(8,128)}, u32[]{:S(2)}, u32[]{:S(2)}) collective-permute-start(f32[74,8,128]{2,1,0:T(8,128)} %slice.42), channel_id=1, source_target_pairs={{0,96},{1,131},{4,100},{5,135},{8,104},{9,139},{12,108},{13,143},{... | collective-permute-start | bytes 909320 | tf_op jit(solution)/shard_map/ppermute | solution.py:49
  33.3 8.3 %collective-permute-start.14 = (f32[74,8,128]{2,1,0:T(8,128)}, f32[74,8,128]{2,1,0:T(8,128)}, u32[]{:S(2)}, u32[]{:S(2)}) collective-permute-start(f32[74,8,128]{2,1,0:T(8,128)} %slice.41), channel_id=1, source_target_pairs={{0,32},{1,129},{4,36},{5,133},{8,40},{9,137},{12,44},{13,141},{16,... | collective-permute-start | bytes 909320 | tf_op jit(solution)/shard_map/ppermute | solution.py:49
  52.0 8.0 %collective-permute-start.27 = (f32[64,1152]{1,0:T(8,128)S(1)}, f32[64,1152]{1,0:T(8,128)S(1)}, u32[]{:S(2)}, u32[]{:S(2)}) collective-permute-start(f32[64,1152]{1,0:T(8,128)S(1)} %get-tuple-element.40), channel_id=1, source_target_pairs={{0,32},{1,129},{4,36},{5,133},{8,40},{9,137},{12,44},{13,141},{16,... | collective-permute-start | bytes 884744 | tf_op jit(solution)/shard_map/ppermute | solution.py:49
  52.7 14.0 %collective-permute-start.16 = (f32[73,8,128]{2,1,0:T(8,128)S(1)}, f32[73,8,128]{2,1,0:T(8,128)S(1)}, u32[]{:S(2)}, u32[]{:S(2)}) collective-permute-start(f32[73,8,128]{2,1,0:T(8,128)S(1)} %get-tuple-element.27), channel_id=1, source_target_pairs={{0,1},{1,0},{4,5},{5,4},{8,9},{9,8},{12,13},{13,12},{16,17},{17,16... | collective-permute-start | bytes 897032 | tf_op jit(solution)/shard_map/ppermute | solution.py:49
  55.1 11.1 %collective-permute-start.17 = (f32[73,8,128]{2,1,0:T(8,128)S(1)}, f32[73,8,128]{2,1,0:T(8,128)S(1)}, u32[]{:S(2)}, u32[]{:S(2)}) collective-permute-start(f32[73,8,128]{2,1,0:T(8,128)S(1)} %get-tuple-element.29), channel_id=1, source_target_pairs={{0,1},{1,0},{4,5},{5,4},{8,9},{9,8},{12,13},{13,12},{16,17},{17,16... | collective-permute-start | bytes 897032 | tf_op jit(solution)/shard_map/ppermute | solution.py:49
  55.1 7.3 %collective-permute-start.25 = (f32[64,1152]{1,0:T(8,128)S(1)}, f32[64,1152]{1,0:T(8,128)S(1)}, u32[]{:S(2)}, u32[]{:S(2)}) collective-permute-start(f32[64,1152]{1,0:T(8,128)S(1)} %get-tuple-element.38), channel_id=1, source_target_pairs={{0,96},{1,131},{4,100},{5,135},{8,104},{9,139},{12,108},{13,143},{... | collective-permute-start | bytes 884744 | tf_op jit(solution)/shard_map/ppermute | solution.py:49
  58.5 8.1 %collective-permute-start.21 = (f32[73,8,128]{2,1,0:T(8,128)S(1)}, f32[73,8,128]{2,1,0:T(8,128)S(1)}, u32[]{:S(2)}, u32[]{:S(2)}) collective-permute-start(f32[73,8,128]{2,1,0:T(8,128)S(1)} %pad_add_fusion.2), channel_id=1, source_target_pairs={{0,28},{1,5},{4,0},{5,9},{8,4},{9,13},{12,8},{13,17},{16,12},{17,2... | collective-permute-start | bytes 897032 | tf_op jit(solution)/shard_map/ppermute | solution.py:49
  60.1 14.7 %collective-permute-start.28 = (f32[128,1152]{1,0:T(8,128)S(1)}, f32[128,1152]{1,0:T(8,128)S(1)}, u32[]{:S(2)}, u32[]{:S(2)}) collective-permute-start(f32[128,1152]{1,0:T(8,128)S(1)} %pad_add_fusion), channel_id=1, source_target_pairs={{0,32},{1,129},{4,36},{5,133},{8,40},{9,137},{12,44},{13,141},{16,... | collective-permute-start | bytes 1769480 | tf_op jit(solution)/shard_map/ppermute | solution.py:49
  62.4 12.4 %collective-permute-start.26 = (f32[128,1152]{1,0:T(8,128)S(1)}, f32[128,1152]{1,0:T(8,128)S(1)}, u32[]{:S(2)}, u32[]{:S(2)}) collective-permute-start(f32[128,1152]{1,0:T(8,128)S(1)} %pad_add_fusion.1), channel_id=1, source_target_pairs={{0,96},{1,131},{4,100},{5,135},{8,104},{9,139},{12,108},{13,143},{... | collective-permute-start | bytes 1769480 | tf_op jit(solution)/shard_map/ppermute | solution.py:49
  66.6 8.1 %collective-permute-start.22 = (f32[73,8,128]{2,1,0:T(8,128)S(1)}, f32[73,8,128]{2,1,0:T(8,128)S(1)}, u32[]{:S(2)}, u32[]{:S(2)}) collective-permute-start(f32[73,8,128]{2,1,0:T(8,128)S(1)} %add_add_fusion.1), channel_id=1, source_target_pairs={{0,28},{1,5},{4,0},{5,9},{8,4},{9,13},{12,8},{13,17},{16,12},{17,2... | collective-permute-start | bytes 897032 | tf_op jit(solution)/shard_map/ppermute | solution.py:49
  74.7 8.1 %collective-permute-start.23 = (f32[73,8,128]{2,1,0:T(8,128)S(1)}, f32[73,8,128]{2,1,0:T(8,128)S(1)}, u32[]{:S(2)}, u32[]{:S(2)}) collective-permute-start(f32[73,8,128]{2,1,0:T(8,128)S(1)} %add_add_fusion.2), channel_id=1, source_target_pairs={{0,28},{1,5},{4,0},{5,9},{8,4},{9,13},{12,8},{13,17},{16,12},{17,2... | collective-permute-start | bytes 897032 | tf_op jit(solution)/shard_map/ppermute | solution.py:49
  85.3 11.1 %collective-permute-start.30 = (f32[32,1152]{1,0:T(8,128)S(1)}, f32[32,1152]{1,0:T(8,128)S(1)}, u32[]{:S(2)}, u32[]{:S(2)}) collective-permute-start(f32[32,1152]{1,0:T(8,128)S(1)} %get-tuple-element.43), channel_id=1, source_target_pairs={{0,128},{1,33},{4,132},{5,37},{8,136},{9,41},{12,140},{13,45},{16,... | collective-permute-start | bytes 442376 | tf_op jit(solution)/shard_map/ppermute | solution.py:49
  85.3 11.1 %collective-permute-start.31 = (f32[32,1152]{1,0:T(8,128)S(1)}, f32[32,1152]{1,0:T(8,128)S(1)}, u32[]{:S(2)}, u32[]{:S(2)}) collective-permute-start(f32[32,1152]{1,0:T(8,128)S(1)} %get-tuple-element.44), channel_id=1, source_target_pairs={{0,2},{1,65},{4,6},{5,69},{8,10},{9,73},{12,14},{13,77},{16,18},{1... | collective-permute-start | bytes 442376 | tf_op jit(solution)/shard_map/ppermute | solution.py:49
  89.5 14.7 %all-to-all-start = ((f32[16,8,128]{2,1,0:T(8,128)}), f32[16,8,128]{2,1,0:T(8,128)S(1)}, u32[]{:S(2)}, u32[]{:S(2)}) async-start(f32[16,8,128]{2,1,0:T(8,128)} %broadcast_in_dim.3), calls=%async_computation | async-start | bytes 131072 | tf_op jit(solution)/shard_map/all_to_all | solution.py:301
  (10 other events, 39.2 us)
where the time goes:
time: 105 us
  starting transfers between devices  48.4 us (46%)
  waiting for transfers between devices  38 us (36%)
  Pallas kernels  11.2 us (11%)
  local copies, waits for them, and re-layouts  3.3 us (3%)
  between operations  2.17 us (2%)
  other arithmetic  1.9 us (2%)
    ppermute x32, starting transfers between devices, send(): return lax.ppermute(block, AXES, route)  41.4 us
    ppermute x32, waiting for transfers between devices, send(): return lax.ppermute(block, AXES, route)  31 us
    pallas_call x1, Pallas kernels, shards(): pl.pallas_call(lambda *refs: visit(PIECES, range(N_TEXT), *refs), out_sha...  8.79 us
    all_to_all x1, starting transfers between devices, shards(): lax.all_to_all(jnp.broadcast_to(sums, (NX * NY, 8, 128)), AXES, 0, 0, axi...  6.99 us
    all_to_all x1, waiting for transfers between devices, shards(): lax.all_to_all(jnp.broadcast_to(sums, (NX * NY, 8, 128)), AXES, 0, 0, axi...  6.95 us
  transfers between devices with their start and end apart: 33, of which 15 were waited for; matrix products, arithmetic and copies ran while one was open for 4% of the time, Pallas kernels for 1%

commit v1 on v0

--- a/solution.py
+++ b/solution.py
@@ -180,7 +180,7 @@
     gradients(image_pieces, text_pieces, (ih, il, th, tl, wh, wl), sums, outs)
 
 
-def unpack(kept_ref, came_ref, other_ref, after_ref, rows_out, sums_out):
+def unpack(kept_ref, came_ref, other_ref, rows_out, sums_out):
     for r in range(ROWS // 8):
         for c in range(COLS):
             at = r * COLS + c
@@ -293,15 +293,13 @@
     grad_image, sums = pl.pallas_call(
         unpack,
         out_shape=(rows_of(ROWS), jax.ShapeDtypeStruct((8, 128), F32)),
-        in_specs=vmem(3) + [pl.BlockSpec(memory_space=pl.ANY)],
+        in_specs=vmem(3),
         out_specs=tuple(vmem(2)),
         compiler_params=pltpu.CompilerParams(vmem_limit_bytes=2 * 2**20),
-    )(gc, w1, other, ra)
-    lines = [[spot(x, y, z, c) for x in range(NX) for y in range(NY)] for z in range(NZ) for c in range(2)]
-    every = lax.all_to_all(
-        jnp.broadcast_to(sums, (NX * NY, 8, 128)), AXES, 0, 0, axis_index_groups=lines, tiled=True
-    )
-    statistics = jnp.sum(every[:, :6].reshape(NX * NY, 3, 256), axis=(0, 2)) * (2.0**-26)
+    )(gc, w1, other)
+    for route in (first, second):
+        sums = (sums + send(sums, route(2))) + (send(sums, route(1)) + send(sums, route(-1)))
+    statistics = jnp.sum(sums[:6].reshape(3, 256), axis=1) * (2.0**-26)
     return grad_image, grad_text, statistics
 
 

time: 105 us -> 103 us (0.981)
  waiting for transfers between devices: 38 us -> 35.5 us
    ppermute x32 -> x38, starting transfers between devices: 41.4 us -> 48.7 us  [send(): return lax.ppermute(block, AXES, route)]
    all_to_all x1 -> x0, starting transfers between devices: 6.99 us -> none  [shards(): lax.all_to_all(jnp.broadcast_to(sums, (NX * NY, 8, 128)), AXES, 0, 0, axi...]
    all_to_all x1 -> x0, waiting for transfers between devices: 6.95 us -> none  [shards(): lax.all_to_all(jnp.broadcast_to(sums, (NX * NY, 8, 128)), AXES, 0, 0, axi...]
    ppermute x32 -> x38, waiting for transfers between devices: 31 us -> 35.5 us  [send(): return lax.ppermute(block, AXES, route)]
  transfers between devices with their start and end apart: 33 -> 38, of which waited for: 15 -> 16; matrix products, arithmetic and copies ran while one was open for 4% -> 4% of each run, Pallas kernels for 1% -> 0%
where the time goes in v1:
time: 103 us; the launch traced here: 102 us
  starting transfers between devices  48.7 us (47%)
  waiting for transfers between devices  35.5 us (34%)
  Pallas kernels  11.2 us (11%)
  local copies, waits for them, and re-layouts  2.63 us (3%)
  between operations  2.18 us (2%)
  other arithmetic  1.91 us (2%)
    ppermute x38, starting transfers between devices, send(): return lax.ppermute(block, AXES, route)  48.7 us
    ppermute x38, waiting for transfers between devices, send(): return lax.ppermute(block, AXES, route)  35.5 us
    pallas_call x1, Pallas kernels, shards(): pl.pallas_call(lambda *refs: visit(PIECES, range(N_TEXT), *refs), out_sha...  8.79 us
  transfers between devices with their start and end apart: 38, of which 16 were waited for; matrix products, arithmetic and copies ran while one was open for 4% of the time, Pallas kernels for 0%

profile of v1, /device:TPU:96, one launch (start us, length us, event | category | flops | bytes accessed | tf_op | source)
XLA Modules:
  0.0 102.1 jit_solution(18181979933984414258)
XLA Ops:
  0.6 1.7 %shard_map.85 = (f32[37,8,128]{2,1,0:T(8,128)}, f32[37,8,128]{2,1,0:T(8,128)}) custom-call(f32[32,1152]{1,0:T(8,128)} %image_ref.1, f32[32,1152]{1,0:T(8,128)} %text_ref.1, s32[1,32]{1,0:T(1,128)} %bitcast.7, s32[1,32]{1,0:T(1,128)} %bitcast.8), custom_call_target="tpu_custom_call" | custom-call | tf_op jit(solution)/shard_map/pallas_call | solution.py:230
  2.4 3.0 %collective-permute-start.11 = (f32[37,8,128]{2,1,0:T(8,128)}, f32[37,8,128]{2,1,0:T(8,128)S(1)}, u32[]{:S(2)}, u32[]{:S(2)}) collective-permute-start(f32[37,8,128]{2,1,0:T(8,128)} %get-tuple-element.24), channel_id=1, source_target_pairs={{0,2},{1,65},{4,6},{5,69},{8,10},{9,73},{12,14},{13,77},{16,18},{1... | collective-permute-start | bytes 454664 | tf_op jit(solution)/shard_map/ppermute | solution.py:49
  9.0 3.2 %collective-permute-start.1 = (f32[74,8,128]{2,1,0:T(8,128)S(1)}, f32[74,8,128]{2,1,0:T(8,128)S(1)}, u32[]{:S(2)}, u32[]{:S(2)}) collective-permute-start(f32[74,8,128]{2,1,0:T(8,128)S(1)} %constant_dynamic-update-slice_fusion.refs_3_), channel_id=1, source_target_pairs={{0,4},{1,29},{4,8},{5,1},{8,12},{9,5},{12,16},{13,9},{16,20},{17,1... | collective-permute-start | bytes 909320 | tf_op jit(solution)/shard_map/ppermute | solution.py:49
  13.2 3.1 %collective-permute-start.13 = (f32[148,8,128]{2,1,0:T(8,128)S(1)}, f32[148,8,128]{2,1,0:T(8,128)S(1)}, u32[]{:S(2)}, u32[]{:S(2)}) collective-permute-start(f32[148,8,128]{2,1,0:T(8,128)S(1)} %constant_dynamic-update-slice_fusion.2.refs_12_), channel_id=1, source_target_pairs={{0,96},{1,131},{4,100},{5,135},{8,104},{9,139},{12,108},{13,143},{... | collective-permute-start | bytes 1818632 | tf_op jit(solution)/shard_map/ppermute | solution.py:49
  16.5 3.7 %collective-permute-start.2 = (f32[74,8,128]{2,1,0:T(8,128)S(1)}, f32[74,8,128]{2,1,0:T(8,128)S(1)}, u32[]{:S(2)}, u32[]{:S(2)}) collective-permute-start(f32[74,8,128]{2,1,0:T(8,128)S(1)} %collective-permute-done.1.refs_4_), channel_id=1, source_target_pairs={{0,4},{1,29},{4,8},{5,1},{8,12},{9,5},{12,16},{13,9},{16,20},{17,1... | collective-permute-start | bytes 909320 | tf_op jit(solution)/shard_map/ppermute | solution.py:49
  20.2 4.3 %collective-permute-done.2.refs_5_ = f32[74,8,128]{2,1,0:T(8,128)S(1)} collective-permute-done((f32[74,8,128]{2,1,0:T(8,128)S(1)}, f32[74,8,128]{2,1,0:T(8,128)S(1)}, u32[]{:S(2)}, u32[]{:S(2)}) %collective-permute-start.2) | collective-permute-done | bytes 303136 | tf_op jit(solution)/shard_map/ppermute | solution.py:49
  24.6 3.7 %collective-permute-start.3 = (f32[74,8,128]{2,1,0:T(8,128)S(1)}, f32[74,8,128]{2,1,0:T(8,128)S(1)}, u32[]{:S(2)}, u32[]{:S(2)}) collective-permute-start(f32[74,8,128]{2,1,0:T(8,128)S(1)} %collective-permute-done.2.refs_5_), channel_id=1, source_target_pairs={{0,4},{1,29},{4,8},{5,1},{8,12},{9,5},{12,16},{13,9},{16,20},{17,1... | collective-permute-start | bytes 909320 | tf_op jit(solution)/shard_map/ppermute | solution.py:49
  29.5 3.0 %collective-permute-start.15 = (f32[74,8,128]{2,1,0:T(8,128)}, f32[74,8,128]{2,1,0:T(8,128)}, u32[]{:S(2)}, u32[]{:S(2)}) collective-permute-start(f32[74,8,128]{2,1,0:T(8,128)} %slice.42), channel_id=1, source_target_pairs={{0,96},{1,131},{4,100},{5,135},{8,104},{9,139},{12,108},{13,143},{... | collective-permute-start | bytes 909320 | tf_op jit(solution)/shard_map/ppermute | solution.py:49
  33.3 3.1 %collective-permute-start.4 = (f32[37,8,128]{2,1,0:T(8,128)S(1)}, f32[37,8,128]{2,1,0:T(8,128)S(1)}, u32[]{:S(2)}, u32[]{:S(2)}) collective-permute-start(f32[37,8,128]{2,1,0:T(8,128)S(1)} %slice.40), channel_id=1, source_target_pairs={{0,4},{1,29},{4,8},{5,1},{8,12},{9,5},{12,16},{13,9},{16,20},{17,1... | collective-permute-start | bytes 454664 | tf_op jit(solution)/shard_map/ppermute | solution.py:49
  36.4 2.7 %collective-permute-done.4.refs_7_ = f32[37,8,128]{2,1,0:T(8,128)S(1)} collective-permute-done((f32[37,8,128]{2,1,0:T(8,128)S(1)}, f32[37,8,128]{2,1,0:T(8,128)S(1)}, u32[]{:S(2)}, u32[]{:S(2)}) %collective-permute-start.4) | collective-permute-done | bytes 151584 | tf_op jit(solution)/shard_map/ppermute | solution.py:49
  41.6 8.8 %shard_map.86 = (f32[8,128]{1,0:T(8,128)}, f32[73,8,128]{2,1,0:T(8,128)S(1)}, f32[73,8,128]{2,1,0:T(8,128)S(1)}, f32[73,8,128]{2,1,0:T(8,128)S(1)}, f32[73,8,128...) custom-call(f32[1,1]{1,0:T(1,128)} %bitcast.5.refs_0_, ...), custom_call_target="tpu_custom_call" | custom-call | flops 5435817984 | bytes 4718592 | tf_op jit(solution)/shard_map/pallas_call | solution.py:257
  52.6 2.4 %collective-permute-start.16 = (f32[73,8,128]{2,1,0:T(8,128)S(1)}, f32[73,8,128]{2,1,0:T(8,128)S(1)}, u32[]{:S(2)}, u32[]{:S(2)}) collective-permute-start(f32[73,8,128]{2,1,0:T(8,128)S(1)} %get-tuple-element.27), channel_id=1, source_target_pairs={{0,1},{1,0},{4,5},{5,4},{8,9},{9,8},{12,13},{13,12},{16,17},{17,16... | collective-permute-start | bytes 897032 | tf_op jit(solution)/shard_map/ppermute | solution.py:49
  55.1 3.0 %collective-permute-start.25 = (f32[64,1152]{1,0:T(8,128)S(1)}, f32[64,1152]{1,0:T(8,128)S(1)}, u32[]{:S(2)}, u32[]{:S(2)}) collective-permute-start(f32[64,1152]{1,0:T(8,128)S(1)} %get-tuple-element.39), channel_id=1, source_target_pairs={{0,96},{1,131},{4,100},{5,135},{8,104},{9,139},{12,108},{13,143},{... | collective-permute-start | bytes 884744 | tf_op jit(solution)/shard_map/ppermute | solution.py:49
  58.5 1.5 %collective-permute-done.27 = f32[64,1152]{1,0:T(8,128)S(1)} collective-permute-done((f32[64,1152]{1,0:T(8,128)S(1)}, f32[64,1152]{1,0:T(8,128)S(1)}, u32[]{:S(2)}, u32[]{:S(2)}) %collective-permute-start.27) | collective-permute-done | bytes 294944 | tf_op jit(solution)/shard_map/ppermute | solution.py:49
  60.4 6.1 %collective-permute-done.21 = f32[73,8,128]{2,1,0:T(8,128)S(1)} collective-permute-done((f32[73,8,128]{2,1,0:T(8,128)S(1)}, f32[73,8,128]{2,1,0:T(8,128)S(1)}, u32[]{:S(2)}, u32[]{:S(2)}) %collective-permute-start.21) | collective-permute-done | bytes 299040 | tf_op jit(solution)/shard_map/ppermute | solution.py:49
  66.7 2.6 %collective-permute-start.26 = (f32[128,1152]{1,0:T(8,128)S(1)}, f32[128,1152]{1,0:T(8,128)S(1)}, u32[]{:S(2)}, u32[]{:S(2)}) collective-permute-start(f32[128,1152]{1,0:T(8,128)S(1)} %pad_add_fusion.1), channel_id=1, source_target_pairs={{0,96},{1,131},{4,100},{5,135},{8,104},{9,139},{12,108},{13,143},{... | collective-permute-start | bytes 1769480 | tf_op jit(solution)/shard_map/ppermute | solution.py:49
  69.2 5.3 %collective-permute-done.22 = f32[73,8,128]{2,1,0:T(8,128)S(1)} collective-permute-done((f32[73,8,128]{2,1,0:T(8,128)S(1)}, f32[73,8,128]{2,1,0:T(8,128)S(1)}, u32[]{:S(2)}, u32[]{:S(2)}) %collective-permute-start.22) | collective-permute-done | bytes 299040 | tf_op jit(solution)/shard_map/ppermute | solution.py:49
  74.7 8.0 %collective-permute-done.23.came_ref = f32[73,8,128]{2,1,0:T(8,128)S(1)} collective-permute-done((f32[73,8,128]{2,1,0:T(8,128)S(1)}, f32[73,8,128]{2,1,0:T(8,128)S(1)}, u32[]{:S(2)}, u32[]{:S(2)}) %collective-permute-start.23) | collective-permute-done | bytes 299040 | tf_op jit(solution)/shard_map/ppermute | solution.py:49
  84.9 2.4 %collective-permute-start.34 = (f32[8,128]{1,0:T(8,128)S(1)}, f32[8,128]{1,0:T(8,128)S(1)}, u32[]{:S(2)}, u32[]{:S(2)}) collective-permute-start(f32[8,128]{1,0:T(8,128)S(1)} %get-tuple-element.42), channel_id=1, source_target_pairs={{0,130},{1,97},{4,134},{5,101},{8,138},{9,105},{12,142},{13,109},{... | collective-permute-start | bytes 12296 | tf_op jit(solution)/shard_map/ppermute | solution.py:49
  87.2 2.6 %collective-permute-start.32 = (f32[8,128]{1,0:T(8,128)S(1)}, f32[8,128]{1,0:T(8,128)S(1)}, u32[]{:S(2)}, u32[]{:S(2)}) collective-permute-start(f32[8,128]{1,0:T(8,128)S(1)} %get-tuple-element.42), channel_id=1, source_target_pairs={{0,2},{1,65},{4,6},{5,69},{8,10},{9,73},{12,14},{13,77},{16,18},{1... | collective-permute-start | bytes 12296 | tf_op jit(solution)/shard_map/ppermute | solution.py:49
  90.6 2.9 %collective-permute-start.31 = (f32[32,1152]{1,0:T(8,128)S(1)}, f32[32,1152]{1,0:T(8,128)S(1)}, u32[]{:S(2)}, u32[]{:S(2)}) collective-permute-start(f32[32,1152]{1,0:T(8,128)S(1)} %get-tuple-element.44), channel_id=1, source_target_pairs={{0,2},{1,65},{4,6},{5,69},{8,10},{9,73},{12,14},{13,77},{16,18},{1... | collective-permute-start | bytes 442376 | tf_op jit(solution)/shard_map/ppermute | solution.py:49
  93.5 2.5 %collective-permute-start.37 = (f32[8,128]{1,0:T(8,128)S(1)}, f32[8,128]{1,0:T(8,128)S(1)}, u32[]{:S(2)}, u32[]{:S(2)}) collective-permute-start(f32[8,128]{1,0:T(8,128)S(1)} %add_add_fusion.4), channel_id=1, source_target_pairs={{0,96},{1,131},{4,100},{5,135},{8,104},{9,139},{12,108},{13,143},{... | collective-permute-start | bytes 12296 | tf_op jit(solution)/shard_map/ppermute | solution.py:49
  96.1 2.2 %collective-permute-start.35 = (f32[8,128]{1,0:T(8,128)S(1)}, f32[8,128]{1,0:T(8,128)S(1)}, u32[]{:S(2)}, u32[]{:S(2)}) collective-permute-start(f32[8,128]{1,0:T(8,128)S(1)} %add_add_fusion.4), channel_id=1, source_target_pairs={{0,64},{1,3},{4,68},{5,7},{8,72},{9,11},{12,76},{13,15},{16,80},{1... | collective-permute-start | bytes 12296 | tf_op jit(solution)/shard_map/ppermute | solution.py:49
  98.3 1.7 %collective-permute-done.30 = f32[32,1152]{1,0:T(8,128)S(1)} collective-permute-done((f32[32,1152]{1,0:T(8,128)S(1)}, f32[32,1152]{1,0:T(8,128)S(1)}, u32[]{:S(2)}, u32[]{:S(2)}) %collective-permute-start.30) | collective-permute-done | bytes 147488 | tf_op jit(solution)/shard_map/ppermute | solution.py:49
  (83 shorter events, 16.4 us)
Async XLA Ops:
  2.4 10.8 %collective-permute-start.11 = (f32[37,8,128]{2,1,0:T(8,128)}, f32[37,8,128]{2,1,0:T(8,128)S(1)}, u32[]{:S(2)}, u32[]{:S(2)}) collective-permute-start(f32[37,8,128]{2,1,0:T(8,128)} %get-tuple-element.24), channel_id=1, source_target_pairs={{0,2},{1,65},{4,6},{5,69},{8,10},{9,73},{12,14},{13,77},{16,18},{1... | collective-permute-start | bytes 454664 | tf_op jit(solution)/shard_map/ppermute | solution.py:49
  5.4 7.8 %collective-permute-start.10 = (f32[37,8,128]{2,1,0:T(8,128)}, f32[37,8,128]{2,1,0:T(8,128)S(1)}, u32[]{:S(2)}, u32[]{:S(2)}) collective-permute-start(f32[37,8,128]{2,1,0:T(8,128)} %get-tuple-element.24), channel_id=1, source_target_pairs={{0,130},{1,97},{4,134},{5,101},{8,138},{9,105},{12,142},{13,109},{... | collective-permute-start | bytes 454664 | tf_op jit(solution)/shard_map/ppermute | solution.py:49
  6.5 6.6 %collective-permute-start.9 = (f32[37,8,128]{2,1,0:T(8,128)}, f32[37,8,128]{2,1,0:T(8,128)S(1)}, u32[]{:S(2)}, u32[]{:S(2)}) collective-permute-start(f32[37,8,128]{2,1,0:T(8,128)} %get-tuple-element.24), channel_id=1, source_target_pairs={{0,128},{1,33},{4,132},{5,37},{8,136},{9,41},{12,140},{13,45},{16,... | collective-permute-start | bytes 454664 | tf_op jit(solution)/shard_map/ppermute | solution.py:49
  9.0 7.5 %collective-permute-start.1 = (f32[74,8,128]{2,1,0:T(8,128)S(1)}, f32[74,8,128]{2,1,0:T(8,128)S(1)}, u32[]{:S(2)}, u32[]{:S(2)}) collective-permute-start(f32[74,8,128]{2,1,0:T(8,128)S(1)} %constant_dynamic-update-slice_fusion.refs_3_), channel_id=1, source_target_pairs={{0,4},{1,29},{4,8},{5,1},{8,12},{9,5},{12,16},{13,9},{16,20},{17,1... | collective-permute-start | bytes 909320 | tf_op jit(solution)/shard_map/ppermute | solution.py:49
  13.2 15.6 %collective-permute-start.13 = (f32[148,8,128]{2,1,0:T(8,128)S(1)}, f32[148,8,128]{2,1,0:T(8,128)S(1)}, u32[]{:S(2)}, u32[]{:S(2)}) collective-permute-start(f32[148,8,128]{2,1,0:T(8,128)S(1)} %constant_dynamic-update-slice_fusion.2.refs_12_), channel_id=1, source_target_pairs={{0,96},{1,131},{4,100},{5,135},{8,104},{9,139},{12,108},{13,143},{... | collective-permute-start | bytes 1818632 | tf_op jit(solution)/shard_map/ppermute | solution.py:49
  16.3 16.2 %collective-permute-start.12 = (f32[148,8,128]{2,1,0:T(8,128)S(1)}, f32[148,8,128]{2,1,0:T(8,128)S(1)}, u32[]{:S(2)}, u32[]{:S(2)}) collective-permute-start(f32[148,8,128]{2,1,0:T(8,128)S(1)} %constant_dynamic-update-slice_fusion.2.refs_12_), channel_id=1, source_target_pairs={{0,32},{1,129},{4,36},{5,133},{8,40},{9,137},{12,44},{13,141},{16,... | collective-permute-start | bytes 1818632 | tf_op jit(solution)/shard_map/ppermute | solution.py:49
  16.5 8.0 %collective-permute-start.2 = (f32[74,8,128]{2,1,0:T(8,128)S(1)}, f32[74,8,128]{2,1,0:T(8,128)S(1)}, u32[]{:S(2)}, u32[]{:S(2)}) collective-permute-start(f32[74,8,128]{2,1,0:T(8,128)S(1)} %collective-permute-done.1.refs_4_), channel_id=1, source_target_pairs={{0,4},{1,29},{4,8},{5,1},{8,12},{9,5},{12,16},{13,9},{16,20},{17,1... | collective-permute-start | bytes 909320 | tf_op jit(solution)/shard_map/ppermute | solution.py:49
  24.6 8.7 %collective-permute-start.3 = (f32[74,8,128]{2,1,0:T(8,128)S(1)}, f32[74,8,128]{2,1,0:T(8,128)S(1)}, u32[]{:S(2)}, u32[]{:S(2)}) collective-permute-start(f32[74,8,128]{2,1,0:T(8,128)S(1)} %collective-permute-done.2.refs_5_), channel_id=1, source_target_pairs={{0,4},{1,29},{4,8},{5,1},{8,12},{9,5},{12,16},{13,9},{16,20},{17,1... | collective-permute-start | bytes 909320 | tf_op jit(solution)/shard_map/ppermute | solution.py:49
  28.3 8.1 %collective-permute-start.5 = (f32[74,8,128]{2,1,0:T(8,128)S(1)}, f32[74,8,128]{2,1,0:T(8,128)S(1)}, u32[]{:S(2)}, u32[]{:S(2)}) collective-permute-start(f32[74,8,128]{2,1,0:T(8,128)S(1)} %collective-permute-done.1.refs_4_), channel_id=1, source_target_pairs={{0,1},{1,0},{4,5},{5,4},{8,9},{9,8},{12,13},{13,12},{16,17},{17,16... | collective-permute-start | bytes 909320 | tf_op jit(solution)/shard_map/ppermute | solution.py:49
  28.3 12.1 %collective-permute-start.6 = (f32[74,8,128]{2,1,0:T(8,128)S(1)}, f32[74,8,128]{2,1,0:T(8,128)}, u32[]{:S(2)}, u32[]{:S(2)}) collective-permute-start(f32[74,8,128]{2,1,0:T(8,128)S(1)} %collective-permute-done.2.refs_5_), channel_id=1, source_target_pairs={{0,1},{1,0},{4,5},{5,4},{8,9},{9,8},{12,13},{13,12},{16,17},{17,16... | collective-permute-start | bytes 909320 | tf_op jit(solution)/shard_map/ppermute | solution.py:49
  29.5 10.9 %collective-permute-start.15 = (f32[74,8,128]{2,1,0:T(8,128)}, f32[74,8,128]{2,1,0:T(8,128)}, u32[]{:S(2)}, u32[]{:S(2)}) collective-permute-start(f32[74,8,128]{2,1,0:T(8,128)} %slice.42), channel_id=1, source_target_pairs={{0,96},{1,131},{4,100},{5,135},{8,104},{9,139},{12,108},{13,143},{... | collective-permute-start | bytes 909320 | tf_op jit(solution)/shard_map/ppermute | solution.py:49
  33.3 8.3 %collective-permute-start.14 = (f32[74,8,128]{2,1,0:T(8,128)}, f32[74,8,128]{2,1,0:T(8,128)}, u32[]{:S(2)}, u32[]{:S(2)}) collective-permute-start(f32[74,8,128]{2,1,0:T(8,128)} %slice.41), channel_id=1, source_target_pairs={{0,32},{1,129},{4,36},{5,133},{8,40},{9,137},{12,44},{13,141},{16,... | collective-permute-start | bytes 909320 | tf_op jit(solution)/shard_map/ppermute | solution.py:49
  51.9 6.5 %collective-permute-start.20 = (f32[37,8,128]{2,1,0:T(8,128)S(1)}, f32[37,8,128]{2,1,0:T(8,128)S(1)}, u32[]{:S(2)}, u32[]{:S(2)}) collective-permute-start(f32[37,8,128]{2,1,0:T(8,128)S(1)} %add.76.refs_0_), channel_id=1, source_target_pairs={{0,28},{1,5},{4,0},{5,9},{8,4},{9,13},{12,8},{13,17},{16,12},{17,2... | collective-permute-start | bytes 454664 | tf_op jit(solution)/shard_map/ppermute | solution.py:49
  52.0 8.0 %collective-permute-start.27 = (f32[64,1152]{1,0:T(8,128)S(1)}, f32[64,1152]{1,0:T(8,128)S(1)}, u32[]{:S(2)}, u32[]{:S(2)}) collective-permute-start(f32[64,1152]{1,0:T(8,128)S(1)} %get-tuple-element.41), channel_id=1, source_target_pairs={{0,32},{1,129},{4,36},{5,133},{8,40},{9,137},{12,44},{13,141},{16,... | collective-permute-start | bytes 884744 | tf_op jit(solution)/shard_map/ppermute | solution.py:49
  52.6 16.6 %collective-permute-start.16 = (f32[73,8,128]{2,1,0:T(8,128)S(1)}, f32[73,8,128]{2,1,0:T(8,128)S(1)}, u32[]{:S(2)}, u32[]{:S(2)}) collective-permute-start(f32[73,8,128]{2,1,0:T(8,128)S(1)} %get-tuple-element.27), channel_id=1, source_target_pairs={{0,1},{1,0},{4,5},{5,4},{8,9},{9,8},{12,13},{13,12},{16,17},{17,16... | collective-permute-start | bytes 897032 | tf_op jit(solution)/shard_map/ppermute | solution.py:49
  55.1 11.6 %collective-permute-start.25 = (f32[64,1152]{1,0:T(8,128)S(1)}, f32[64,1152]{1,0:T(8,128)S(1)}, u32[]{:S(2)}, u32[]{:S(2)}) collective-permute-start(f32[64,1152]{1,0:T(8,128)S(1)} %get-tuple-element.39), channel_id=1, source_target_pairs={{0,96},{1,131},{4,100},{5,135},{8,104},{9,139},{12,108},{13,143},{... | collective-permute-start | bytes 884744 | tf_op jit(solution)/shard_map/ppermute | solution.py:49
  58.4 8.1 %collective-permute-start.21 = (f32[73,8,128]{2,1,0:T(8,128)S(1)}, f32[73,8,128]{2,1,0:T(8,128)S(1)}, u32[]{:S(2)}, u32[]{:S(2)}) collective-permute-start(f32[73,8,128]{2,1,0:T(8,128)S(1)} %pad_add_fusion.2), channel_id=1, source_target_pairs={{0,28},{1,5},{4,0},{5,9},{8,4},{9,13},{12,8},{13,17},{16,12},{17,2... | collective-permute-start | bytes 897032 | tf_op jit(solution)/shard_map/ppermute | solution.py:49
  60.1 22.7 %collective-permute-start.28 = (f32[128,1152]{1,0:T(8,128)S(1)}, f32[128,1152]{1,0:T(8,128)S(1)}, u32[]{:S(2)}, u32[]{:S(2)}) collective-permute-start(f32[128,1152]{1,0:T(8,128)S(1)} %pad_add_fusion), channel_id=1, source_target_pairs={{0,32},{1,129},{4,36},{5,133},{8,40},{9,137},{12,44},{13,141},{16,... | collective-permute-start | bytes 1769480 | tf_op jit(solution)/shard_map/ppermute | solution.py:49
  66.5 8.1 %collective-permute-start.22 = (f32[73,8,128]{2,1,0:T(8,128)S(1)}, f32[73,8,128]{2,1,0:T(8,128)S(1)}, u32[]{:S(2)}, u32[]{:S(2)}) collective-permute-start(f32[73,8,128]{2,1,0:T(8,128)S(1)} %add_add_fusion.1), channel_id=1, source_target_pairs={{0,28},{1,5},{4,0},{5,9},{8,4},{9,13},{12,8},{13,17},{16,12},{17,2... | collective-permute-start | bytes 897032 | tf_op jit(solution)/shard_map/ppermute | solution.py:49
  66.7 16.1 %collective-permute-start.26 = (f32[128,1152]{1,0:T(8,128)S(1)}, f32[128,1152]{1,0:T(8,128)S(1)}, u32[]{:S(2)}, u32[]{:S(2)}) collective-permute-start(f32[128,1152]{1,0:T(8,128)S(1)} %pad_add_fusion.1), channel_id=1, source_target_pairs={{0,96},{1,131},{4,100},{5,135},{8,104},{9,139},{12,108},{13,143},{... | collective-permute-start | bytes 1769480 | tf_op jit(solution)/shard_map/ppermute | solution.py:49
  74.6 8.1 %collective-permute-start.23 = (f32[73,8,128]{2,1,0:T(8,128)S(1)}, f32[73,8,128]{2,1,0:T(8,128)S(1)}, u32[]{:S(2)}, u32[]{:S(2)}) collective-permute-start(f32[73,8,128]{2,1,0:T(8,128)S(1)} %add_add_fusion.2), channel_id=1, source_target_pairs={{0,28},{1,5},{4,0},{5,9},{8,4},{9,13},{12,8},{13,17},{16,12},{17,2... | collective-permute-start | bytes 897032 | tf_op jit(solution)/shard_map/ppermute | solution.py:49
  84.9 8.6 %collective-permute-start.34 = (f32[8,128]{1,0:T(8,128)S(1)}, f32[8,128]{1,0:T(8,128)S(1)}, u32[]{:S(2)}, u32[]{:S(2)}) collective-permute-start(f32[8,128]{1,0:T(8,128)S(1)} %get-tuple-element.42), channel_id=1, source_target_pairs={{0,130},{1,97},{4,134},{5,101},{8,138},{9,105},{12,142},{13,109},{... | collective-permute-start | bytes 12296 | tf_op jit(solution)/shard_map/ppermute | solution.py:49
  90.6 7.7 %collective-permute-start.31 = (f32[32,1152]{1,0:T(8,128)S(1)}, f32[32,1152]{1,0:T(8,128)S(1)}, u32[]{:S(2)}, u32[]{:S(2)}) collective-permute-start(f32[32,1152]{1,0:T(8,128)S(1)} %get-tuple-element.44), channel_id=1, source_target_pairs={{0,2},{1,65},{4,6},{5,69},{8,10},{9,73},{12,14},{13,77},{16,18},{1... | collective-permute-start | bytes 442376 | tf_op jit(solution)/shard_map/ppermute | solution.py:49
  93.5 7.1 %collective-permute-start.37 = (f32[8,128]{1,0:T(8,128)S(1)}, f32[8,128]{1,0:T(8,128)S(1)}, u32[]{:S(2)}, u32[]{:S(2)}) collective-permute-start(f32[8,128]{1,0:T(8,128)S(1)} %add_add_fusion.4), channel_id=1, source_target_pairs={{0,96},{1,131},{4,100},{5,135},{8,104},{9,139},{12,108},{13,143},{... | collective-permute-start | bytes 12296 | tf_op jit(solution)/shard_map/ppermute | solution.py:49
  (15 other events, 64.1 us)
